TPU v7x, 256 devices: a whole 4x4x8 slice. The times are simulated.
256 devices in a mesh: dp: 4 (over x), owner: 64 (over z, y, core).
Axes of the slice: x: 4, y: 4, z: 8, core: 2. Of those that a mesh axis runs over, the one named last changes fastest.
Arguments:
- tokens: bfloat16 [32768, 2048], P(('dp', 'owner')), may hold values from -6 to 6
- grads: bfloat16 [32768, 8, 768], P(('dp', 'owner')), may hold values from -0.19921875 to 0.19921875
- routing: int32 [32768, 8], P(('dp', 'owner')), may hold values from 0 to 127, as said below
- basis_in: bfloat16 [64, 2048, 2048], P('owner'), may hold values from -0.125 to 0.125
- basis_out: bfloat16 [64, 768, 768], P('owner'), may hold values from -0.21875 to 0.21875
Outputs:
- eigenvalues: float32 [2048, 64, 768], P('dp', 'owner')
Inputs may be any that keep to these rules, and one draw needn't show every extreme that they name: `routing`: in each device's block of 128 tokens no expert is chosen by more than 16 tokens, and some expert below 64 is chosen by exactly 16 tokens of every block. The 8 experts of one token differ.
All inputs are finite; a program needn't handle non-finite values.
Results may differ from a plain program's by a relative error of at most 0.00048.
Values may be sent and summed in bfloat16 or wider, within the bound.
No kernel may reach another device: no remote copies, remote signals or barrier semaphores. Data moves between devices by JAX's collectives and lax.ppermute only.
A program may use at most 128 MiB of HBM per device.

v0:
```python
import jax
import jax.numpy as jnp
from jax import lax
from jax.sharding import PartitionSpec as P

CAP = 16


def on_device(tokens, grads, routing, basis_in, basis_out):
    tok_dev, width = tokens.shape
    top = routing.shape[1]
    hidden = grads.shape[2]
    exp_dev = basis_in.shape[0]
    owners = lax.axis_size("owner")
    window = exp_dev * owners
    flat = routing.reshape(-1)
    onehot = (flat[:, None] == jnp.arange(window, dtype=jnp.int32)[None, :]).astype(jnp.int32)
    rank = jnp.sum((jnp.cumsum(onehot, axis=0) - onehot) * onehot, axis=1)
    target = jnp.where(flat < window, flat, window)
    in_rows = jnp.repeat(tokens, top, axis=0)
    out_rows = grads.reshape(tok_dev * top, hidden)
    send_in = (
        jnp.zeros((window, CAP, width), jnp.bfloat16).at[target, rank].set(in_rows, mode="drop")
    )
    send_out = (
        jnp.zeros((window, CAP, hidden), jnp.bfloat16).at[target, rank].set(out_rows, mode="drop")
    )
    recv_in, recv_out = (
        lax.all_to_all(send_in, "owner", split_axis=0, concat_axis=1, tiled=True),
        lax.all_to_all(send_out, "owner", split_axis=0, concat_axis=1, tiled=True),
    )
    rotated_out = jnp.einsum(
        "esf,efk->esk", recv_out, basis_out, preferred_element_type=jnp.float32
    )
    g_sq = (rotated_out * rotated_out).astype(jnp.bfloat16)
    rotated_in = jnp.einsum("esd,edk->esk", recv_in, basis_in, preferred_element_type=jnp.float32)
    a_sq = (rotated_in * rotated_in).astype(jnp.bfloat16)
    quarter = lax.all_to_all(a_sq, "dp", split_axis=2, concat_axis=1, tiled=True)
    all_grads = lax.all_gather(g_sq, "dp", axis=1, tiled=True)
    values = jnp.einsum("esd,esf->def", quarter, all_grads, preferred_element_type=jnp.float32)
    return values


def solution(mesh):
    return jax.shard_map(
        on_device,
        mesh=mesh,
        in_specs=(
            P(("dp", "owner"), None),
            P(("dp", "owner"), None, None),
            P(("dp", "owner"), None),
            P("owner", None, None),
            P("owner", None, None),
        ),
        out_specs=P("dp", "owner", None),
        check_vma=False,
    )
```

profile of v0, /device:TPU:56, one launch (start us, length us, event | category | flops | bytes accessed | tf_op | source)
XLA Modules:
  0.0 346.2 jit_solution(4987443988182270449)
XLA Ops:
  6.5 0.0 copy-start
  6.5 0.9 copy.21
  7.4 0.1 eq.29
  7.5 0.1 eq.25
  7.6 0.1 reshape.101
  7.8 0.0 copy-start.2
  7.8 18.0 %reduce-window.6 = s32[64,8,128]{2,1,0:T(8,128)S(1)} reduce-window(s32[64,8,128]{2,1,0:T(8,128)S(1)} %fusion.18, s32[]{:T(128)} %constant.6.clone.1), window={size=1x1x128 pad=0_0x0_0x127_0}, to_apply=%region_0.0 | reduce-window | flops 8323072 | bytes 524292 | tf_op jit(solution)/shard_map/reduce-window
  25.8 0.1 slice.8
  25.9 0.1 copy.24
  26.1 0.1 copy.25
  26.2 0.1 broadcast_add_fusion
  26.3 0.1 fusion.17
  26.4 0.7 multiply_reduce_fusion
  27.2 0.8 and_reduce_fusion
  27.9 0.0 copy-done
  27.9 6.4 %scatter_custom_fusion = bf16[1024,768]{1,0:T(8,128)(2,1)} fusion(s32[1024]{0:T(1024)S(1)} %broadcast_select_fusion, bf16[128,8,768]{2,1,0:T(8,128)(2,1)S(1)} %copy-done, bf16[]{:T(256)} %constant.4.clone.1), kind=kCustom, calls=%fused_computation.11 | custom fusion | bytes 3145730
  34.4 11.4 %all-to-all-start = ((bf16[64,16,768]{2,1,0:T(8,128)(2,1)}), bf16[64,16,768]{2,1,0:T(8,128)(2,1)S(1)}, u32[]{:S(2)}, u32[]{:S(2)}) async-start(bf16[64,16,768]{2,1,0:T(8,128)(2,1)} %bitcast.4), calls=%async_computation | async-start | bytes 3145728 | tf_op jit(solution)/shard_map/all_to_all | solution.py:30
  45.8 0.0 copy-done.2
  45.8 9.0 %scatter_custom_fusion.1 = bf16[1024,2048]{1,0:T(8,128)(2,1)} fusion(s32[1024]{0:T(1024)S(1)} %broadcast_select_fusion, bf16[]{:T(256)} %constant.4.clone.1, bf16[128,2048]{1,0:T(8,128)(2,1)S(1)} %copy-done.2), kind=kCustom, calls=%fused_computation.5 | custom fusion | bytes 4718594
  54.9 30.2 %all-to-all-done = bf16[64,16,768]{2,1,0:T(8,128)(2,1)S(1)} async-done(((bf16[64,16,768]{2,1,0:T(8,128)(2,1)}), bf16[64,16,768]{2,1,0:T(8,128)(2,1)S(1)}, u32[]{:S(2)}, u32[]{:S(2)}) %all-to-all-start) | async-done | bytes 1572896 | tf_op jit(solution)/shard_map/all_to_all | solution.py:30
  85.0 0.0 copy-start.3
  85.0 6.6 %all-to-all-start.1 = ((bf16[64,16,2048]{2,1,0:T(8,128)(2,1)}), bf16[64,16,2048]{2,1,0:T(8,128)(2,1)}, u32[]{:S(2)}, u32[]{:S(2)}) async-start(bf16[64,16,2048]{2,1,0:T(8,128)(2,1)} %bitcast.58), calls=%async_computation.1 | async-start | bytes 8388608 | tf_op jit(solution)/shard_map/all_to_all | solution.py:29
  91.6 0.2 all-gather.3.cloned.1.call-start
  91.9 0.0 copy-done.3
  91.9 2.5 multiply_convert_fusion.1
  94.4 0.0 all-gather.3.cloned.1.call-update
  94.4 92.5 %all-to-all-done.1 = bf16[64,16,2048]{2,1,0:T(8,128)(2,1)} async-done(((bf16[64,16,2048]{2,1,0:T(8,128)(2,1)}), bf16[64,16,2048]{2,1,0:T(8,128)(2,1)}, u32[]{:S(2)}, u32[]{:S(2)}) %all-to-all-start.1) | async-done | bytes 4194336 | tf_op jit(solution)/shard_map/all_to_all | solution.py:29
  187.0 13.9 %fusion.6 = bf16[1,1024,2048]{2,1,0:T(8,128)(2,1)} fusion(bf16[1024,2048]{1,0:T(8,128)(2,1)} %bitcast.9, bf16[1,2048,2048]{2,1,0:T(8,128)(2,1)} %param.8), kind=kOutput, calls=%fused_computation.7 | convolution fusion | flops 8594128896 | bytes 16777216 | tf_op jit(solution)/shard_map/esd,edk->esk/dot_general | solution.py:36
  200.8 20.6 %copy.26 = bf16[1,1024,2048]{1,0,2:T(2,128)(2,1)} copy(bf16[1,1024,2048]{2,1,0:T(8,128)(2,1)} %fusion.6) | data formatting | bytes 8388608 | tf_op jit(solution)/shard_map/convert_element_type | solution.py:37
  221.4 0.5 broadcast.100
  221.9 25.9 %reduce.6 = bf16[2048,1024]{1,0:T(8,128)(2,1)} reduce(bf16[2048,1,1024]{2,1,0:T(2,128)(2,1)} %bitcast.55, bf16[]{:T(256)} %broadcast.100), dimensions={1}, to_apply=%bitcast.49.reduce_sub_computation | reduce | bytes 8388610
  247.9 6.2 %reshape.137 = bf16[4,2,262144]{2,1,0:T(2,128)(2,1)} reshape(bf16[2048,1024]{1,0:T(8,128)(2,1)} %reduce.6) | data formatting | bytes 8388608
  254.1 54.9 %all_to_all.33 = bf16[4,2,262144]{2,1,0:T(2,128)(2,1)} all-to-all(bf16[4,2,262144]{2,1,0:T(2,128)(2,1)} %reshape.137), channel_id=1, replica_groups=mesh['dp'=4,'owner'=64] {'dp'}, dimensions={0} | all-to-all | bytes 8388608 | tf_op jit(solution)/shard_map/all_to_all | solution.py:38
  309.0 7.4 %reshape.138 = bf16[2048,1,1024]{2,1,0:T(2,128)(2,1)} reshape(bf16[4,2,262144]{2,1,0:T(2,128)(2,1)} %all_to_all.33) | data formatting | bytes 8388608
  316.4 7.1 %copy.29 = bf16[1,1024,2048]{1,2,0:T(8,128)(2,1)} copy(bf16[1,1024,2048]{1,0,2:T(2,128)(2,1)} %bitcast.56) | data formatting | bytes 8388608
  323.5 6.2 %copy.27 = bf16[1,4,1024,512]{3,2,1,0:T(8,128)(2,1)} copy(bf16[1,4,1024,512]{2,3,1,0:T(8,128)(2,1)} %bitcast.57) | data formatting | bytes 8388608 | tf_op jit(solution)/shard_map/all_to_all | solution.py:38
  329.7 0.0 all-gather.3.cloned.1.call-done
  329.7 0.0 copy-start.1
  329.7 6.9 %convolution_bitcast_fusion = f32[512,1,768]{0,2,1:T(8,128)S(1)} fusion(bf16[4096,768]{1,0:T(8,128)(2,1)} %all-gather.3.cloned.1.call-done, bf16[4096,512]{1,0:T(8,128)(2,1)} %bitcast.59), kind=kOutput, calls=%fused_computation.13 | convolution fusion | flops 3221225472 | bytes 12058624 | tf_op jit(solution)/shard_map/esd,esf->def/dot_general | solution.py:40
  336.6 2.8 copy.28
  339.4 0.0 copy-done.1
  (5 shorter events, 0.1 us)
Async XLA Ops:
  6.5 21.4 %copy-start = (bf16[128,8,768]{2,1,0:T(8,128)(2,1)S(1)}, bf16[128,8,768]{2,1,0:T(8,128)(2,1)}, u32[]{:S(2)}) copy-start(bf16[128,8,768]{2,1,0:T(8,128)(2,1)} %param.6) | copy-start | bytes 4718596
  7.8 38.1 %copy-start.2 = (bf16[128,2048]{1,0:T(8,128)(2,1)S(1)}, bf16[128,2048]{1,0:T(8,128)(2,1)}, u32[]{:S(2)}) copy-start(bf16[128,2048]{1,0:T(8,128)(2,1)} %param.5) | copy-start | bytes 1572868
  34.4 50.6 %all-to-all-start = ((bf16[64,16,768]{2,1,0:T(8,128)(2,1)}), bf16[64,16,768]{2,1,0:T(8,128)(2,1)S(1)}, u32[]{:S(2)}, u32[]{:S(2)}) async-start(bf16[64,16,768]{2,1,0:T(8,128)(2,1)} %bitcast.4), calls=%async_computation | async-start | bytes 3145728 | tf_op jit(solution)/shard_map/all_to_all | solution.py:30
  85.0 6.8 %copy-start.3 = (bf16[1,768,768]{2,1,0:T(8,128)(2,1)S(1)}, bf16[1,768,768]{2,1,0:T(8,128)(2,1)}, u32[]{:S(2)}) copy-start(bf16[1,768,768]{2,1,0:T(8,128)(2,1)} %param.9) | copy-start | bytes 3538948
  85.0 101.9 %all-to-all-start.1 = ((bf16[64,16,2048]{2,1,0:T(8,128)(2,1)}), bf16[64,16,2048]{2,1,0:T(8,128)(2,1)}, u32[]{:S(2)}, u32[]{:S(2)}) async-start(bf16[64,16,2048]{2,1,0:T(8,128)(2,1)} %bitcast.58), calls=%async_computation.1 | async-start | bytes 8388608 | tf_op jit(solution)/shard_map/all_to_all | solution.py:29
  91.6 238.1 %all-gather.3.cloned.1.call-start = ((), (), s32[]{:S(2)}) async-start(), calls=%async_computation.3 | async-start | bytes 7864320 | tf_op jit(solution)/shard_map/all_gather | solution.py:39
  329.7 9.7 %copy-start.1 = (bf16[128,8,768]{2,1,0:T(8,128)(2,1)S(1)}, bf16[128,8,768]{2,1,0:T(8,128)(2,1)}, u32[]{:S(2)}) copy-start(bf16[128,8,768]{2,1,0:T(8,128)(2,1)} %param.6) | copy-start | bytes 4718596
Sparse Core Ops, SparseCore 0:
  94.6 69.4 all-gather.2
where the time goes:
time: 347 us; the launch traced here: 346 us
  waiting for transfers between devices  123 us (35%)
  local copies, waits for them, and re-layouts  67.8 us (20%)
  blocking collectives  54.9 us (16%)
  other arithmetic  45.7 us (13%)
  matrix products  23.3 us (7%)
  starting transfers between devices  18.3 us (5%)
  between operations  13.5 us (4%)
    all_to_all x1, waiting for transfers between devices, on_device(): lax.all_to_all(send_in, 'owner', split_axis=0, concat_axis=1, tiled=True)  92.5 us
    all_to_all x1, blocking collectives, on_device(): lax.all_to_all(a_sq, 'dp', split_axis=2, concat_axis=1, tiled=True)  54.9 us
    unnamed x15, local copies, waits for them, and re-layouts  37.7 us
    all_to_all x1, waiting for transfers between devices, on_device(): lax.all_to_all(send_out, 'owner', split_axis=0, concat_axis=1, tiled=True)  30.2 us
    unnamed x4, other arithmetic  27.4 us
    convert_element_type x1, local copies, waits for them, and re-layouts, on_device(): a_sq = (rotated_in * rotated_in).astype(jnp.bfloat16)  20.6 us
    another operation x3, other arithmetic  18.2 us
    dot_general x1, matrix products, on_device(): jnp.einsum('esd,edk->esk', recv_in, basis_in, preferred_element_type=jnp....  13.9 us
  transfers between devices with their start and end apart: 3, of which 2 were waited for; matrix products, arithmetic and copies ran while one was open for 29% of the time, Pallas kernels for 0%

commit v1 on v0

--- a/solution.py
+++ b/solution.py
@@ -35,7 +35,9 @@
     g_sq = (rotated_out * rotated_out).astype(jnp.bfloat16)
     rotated_in = jnp.einsum("esd,edk->esk", recv_in, basis_in, preferred_element_type=jnp.float32)
     a_sq = (rotated_in * rotated_in).astype(jnp.bfloat16)
-    quarter = lax.all_to_all(a_sq, "dp", split_axis=2, concat_axis=1, tiled=True)
+    pieces = jnp.split(a_sq, lax.axis_size("dp"), axis=2)
+    incoming = lax.all_to_all(jnp.stack(pieces), "dp", 0, 0)
+    quarter = jnp.concatenate(incoming, axis=1)
     all_grads = lax.all_gather(g_sq, "dp", axis=1, tiled=True)
     values = jnp.einsum("esd,esf->def", quarter, all_grads, preferred_element_type=jnp.float32)
     return values

time: 347 us -> 270 us (0.78)
  local copies, waits for them, and re-layouts: 67.8 us -> 20.7 us
  other arithmetic: 45.7 us -> 20.3 us
    unnamed x4 -> x3, other arithmetic: 27.4 us -> 1.5 us
    unnamed x15 -> x5, local copies, waits for them, and re-layouts: 37.7 us -> 17 us
    convert_element_type x1 -> x0, local copies, waits for them, and re-layouts: 20.6 us -> none  [on_device(): a_sq = (rotated_in * rotated_in).astype(jnp.bfloat16)]
    all_to_all x1 -> x0, local copies, waits for them, and re-layouts: 6.19 us -> none  [on_device(): lax.all_to_all(a_sq, 'dp', split_axis=2, concat_axis=1, tiled=True)]
    another operation x3 -> x4, other arithmetic: 18.2 us -> 18.8 us
  transfers between devices with their start and end apart: 3 -> 3, of which waited for: 2 -> 2; matrix products, arithmetic and copies ran while one was open for 29% -> 10% of each run, Pallas kernels for 0% -> 0%
where the time goes in v1:
time: 270 us
  waiting for transfers between devices  121 us (45%)
  blocking collectives  53.1 us (20%)
  matrix products  23.1 us (9%)
  local copies, waits for them, and re-layouts  20.7 us (8%)
  other arithmetic  20.3 us (8%)
  starting transfers between devices  18.1 us (7%)
  between operations  13.5 us (5%)
    all_to_all x1, waiting for transfers between devices, on_device(): lax.all_to_all(send_in, 'owner', split_axis=0, concat_axis=1, tiled=True)  91.3 us
    all_to_all x1, blocking collectives, on_device(): incoming = lax.all_to_all(jnp.stack(pieces), 'dp', 0, 0)  53.1 us
    all_to_all x1, waiting for transfers between devices, on_device(): lax.all_to_all(send_out, 'owner', split_axis=0, concat_axis=1, tiled=True)  29.6 us
    another operation x3, other arithmetic  18.2 us
    unnamed x5, local copies, waits for them, and re-layouts  17 us
    dot_general x1, matrix products, on_device(): jnp.einsum('esd,edk->esk', recv_in, basis_in, preferred_element_type=jnp....  12.5 us
    all_to_all x1, starting transfers between devices, on_device(): lax.all_to_all(send_out, 'owner', split_axis=0, concat_axis=1, tiled=True)  11.4 us
    dot_general x1, matrix products, on_device(): jnp.einsum('esd,esf->def', quarter, all_grads, preferred_element_type=jnp...  6.8 us
  transfers between devices with their start and end apart: 3, of which 2 were waited for; matrix products, arithmetic and copies ran while one was open for 10% of the time, Pallas kernels for 0%

profile of v1, /device:TPU:56, one launch (start us, length us, event | category | flops | bytes accessed | tf_op | source)
XLA Modules:
  0.0 269.8 jit_solution(853579221567439363)
XLA Ops:
  6.5 0.0 copy-start
  6.5 0.9 copy.7
  7.4 0.1 eq.29
  7.5 0.1 eq.25
  7.6 0.1 reshape.102
  7.8 18.0 %reduce-window.6 = s32[64,8,128]{2,1,0:T(8,128)S(1)} reduce-window(s32[64,8,128]{2,1,0:T(8,128)S(1)} %fusion.18, s32[]{:T(128)} %constant.6.clone.1), window={size=1x1x128 pad=0_0x0_0x127_0}, to_apply=%region_0.0 | reduce-window | flops 8323072 | bytes 524292 | tf_op jit(solution)/shard_map/reduce-window
  25.8 0.1 slice.8
  25.9 0.1 copy.10
  26.1 0.1 copy.11
  26.2 0.1 broadcast_add_fusion
  26.3 0.1 fusion.17
  26.4 0.7 multiply_reduce_fusion
  27.2 0.8 and_reduce_fusion
  27.9 0.0 copy-done
  27.9 6.4 %scatter_custom_fusion = bf16[1024,768]{1,0:T(8,128)(2,1)} fusion(s32[1024]{0:T(1024)S(1)} %broadcast_select_fusion, bf16[128,8,768]{2,1,0:T(8,128)(2,1)S(1)} %copy-done, bf16[]{:T(256)} %constant.4.clone.1), kind=kCustom, calls=%fused_computation.12 | custom fusion | bytes 3145730
  34.4 11.4 %all-to-all-start = ((bf16[64,16,768]{2,1,0:T(8,128)(2,1)}), bf16[64,16,768]{2,1,0:T(8,128)(2,1)S(1)}, u32[]{:S(2)}, u32[]{:S(2)}) async-start(bf16[64,16,768]{2,1,0:T(8,128)(2,1)} %bitcast.4), calls=%async_computation | async-start | bytes 3145728 | tf_op jit(solution)/shard_map/all_to_all | solution.py:30
  45.8 9.6 %scatter_custom_fusion.1 = bf16[1024,2048]{1,0:T(8,128)(2,1)} fusion(s32[1024]{0:T(1024)S(1)} %broadcast_select_fusion, bf16[]{:T(256)} %constant.4.clone.1, bf16[128,2048]{1,0:T(8,128)(2,1)} %param.5), kind=kCustom, calls=%fused_computation.6 | custom fusion | bytes 4718594
  55.4 29.6 %all-to-all-done = bf16[64,16,768]{2,1,0:T(8,128)(2,1)S(1)} async-done(((bf16[64,16,768]{2,1,0:T(8,128)(2,1)}), bf16[64,16,768]{2,1,0:T(8,128)(2,1)S(1)}, u32[]{:S(2)}, u32[]{:S(2)}) %all-to-all-start) | async-done | bytes 1572896 | tf_op jit(solution)/shard_map/all_to_all | solution.py:30
  85.0 6.5 %all-to-all-start.1 = ((bf16[64,16,2048]{2,1,0:T(8,128)(2,1)}), bf16[64,16,2048]{2,1,0:T(8,128)(2,1)}, u32[]{:S(2)}, u32[]{:S(2)}) async-start(bf16[64,16,2048]{2,1,0:T(8,128)(2,1)} %bitcast.58), calls=%async_computation.1 | async-start | bytes 8388608 | tf_op jit(solution)/shard_map/all_to_all | solution.py:29
  91.5 0.2 all-gather.3.cloned.1.call-start
  91.7 3.8 %multiply_convert_fusion.1 = bf16[1024,768]{1,0:T(8,128)(2,1)} fusion(bf16[1024,768]{1,0:T(8,128)(2,1)S(1)} %bitcast.60, bf16[1,768,768]{2,1,0:T(8,128)(2,1)} %param.9), kind=kOutput, calls=%fused_computation.9 | convolution fusion | flops 1209532416 | bytes 4325376 | tf_op jit(solution)/shard_map/esf,efk->esk/dot_general | solution.py:32
  95.5 0.0 all-gather.3.cloned.1.call-update
  95.6 91.3 %all-to-all-done.1 = bf16[64,16,2048]{2,1,0:T(8,128)(2,1)} async-done(((bf16[64,16,2048]{2,1,0:T(8,128)(2,1)}), bf16[64,16,2048]{2,1,0:T(8,128)(2,1)}, u32[]{:S(2)}, u32[]{:S(2)}) %all-to-all-start.1) | async-done | bytes 4194336 | tf_op jit(solution)/shard_map/all_to_all | solution.py:29
  186.8 12.5 %fusion.6 = bf16[1,1024,2048]{2,1,0:T(8,128)(2,1)S(1)} fusion(bf16[1024,2048]{1,0:T(8,128)(2,1)} %bitcast.9, bf16[1,2048,2048]{2,1,0:T(8,128)(2,1)} %param.8), kind=kOutput, calls=%fused_computation.8 | convolution fusion | flops 8594128896 | bytes 16777216 | tf_op jit(solution)/shard_map/esd,edk->esk/dot_general | solution.py:36
  199.3 0.4 slice_bitcast_fusion.3
  199.7 0.6 pad_maximum_fusion
  200.3 53.1 %all_to_all.23 = bf16[4,1,1024,512]{3,2,1,0:T(8,128)(2,1)} all-to-all(bf16[4,1,1024,512]{3,2,1,0:T(8,128)(2,1)S(1)} %pad_maximum_fusion), channel_id=1, replica_groups=mesh['dp'=4,'owner'=64] {'dp'}, dimensions={0} | all-to-all | bytes 8388608 | tf_op jit(solution)/shard_map/all_to_all | solution.py:39
  253.4 0.0 all-gather.3.cloned.1.call-done
  253.4 6.8 %convolution_bitcast_fusion = f32[512,1,768]{0,2,1:T(8,128)S(1)} fusion(bf16[4096,768]{1,0:T(8,128)(2,1)} %all-gather.3.cloned.1.call-done, bf16[4096,512]{1,0:T(8,128)(2,1)} %bitcast.59), kind=kOutput, calls=%fused_computation.14 | convolution fusion | flops 3221225472 | bytes 12058624 | tf_op jit(solution)/shard_map/esd,esf->def/dot_general | solution.py:42
  260.2 2.8 %copy.12 = f32[512,1,768]{2,1,0:T(1,128)} copy(f32[512,1,768]{0,2,1:T(8,128)S(1)} %convolution_bitcast_fusion) | data formatting | bytes 3145728 | tf_op jit(solution)/shard_map/esd,esf->def/transpose | solution.py:42
  (5 shorter events, 0.1 us)
Async XLA Ops:
  6.5 21.4 %copy-start = (bf16[128,8,768]{2,1,0:T(8,128)(2,1)S(1)}, bf16[128,8,768]{2,1,0:T(8,128)(2,1)}, u32[]{:S(2)}) copy-start(bf16[128,8,768]{2,1,0:T(8,128)(2,1)} %param.6) | copy-start | bytes 4718596
  34.4 50.6 %all-to-all-start = ((bf16[64,16,768]{2,1,0:T(8,128)(2,1)}), bf16[64,16,768]{2,1,0:T(8,128)(2,1)S(1)}, u32[]{:S(2)}, u32[]{:S(2)}) async-start(bf16[64,16,768]{2,1,0:T(8,128)(2,1)} %bitcast.4), calls=%async_computation | async-start | bytes 3145728 | tf_op jit(solution)/shard_map/all_to_all | solution.py:30
  85.0 101.8 %all-to-all-start.1 = ((bf16[64,16,2048]{2,1,0:T(8,128)(2,1)}), bf16[64,16,2048]{2,1,0:T(8,128)(2,1)}, u32[]{:S(2)}, u32[]{:S(2)}) async-start(bf16[64,16,2048]{2,1,0:T(8,128)(2,1)} %bitcast.58), calls=%async_computation.1 | async-start | bytes 8388608 | tf_op jit(solution)/shard_map/all_to_all | solution.py:29
  91.5 161.9 %all-gather.3.cloned.1.call-start = ((), (), s32[]{:S(2)}) async-start(), calls=%async_computation.3 | async-start | bytes 7864320 | tf_op jit(solution)/shard_map/all_gather | solution.py:41
Sparse Core Ops, SparseCore 0:
  95.7 69.4 all-gather.2
